TPU v7x, 32 devices: a whole 2x2x4 slice. The times are simulated.
32 devices in a mesh: groups: 2 (over x), replica: 8 (over z, y), tensor: 2 (over core).
Axes of the slice: x: 2, y: 2, z: 4, core: 2. Of those that a mesh axis runs over, the one named last changes fastest.
Arguments:
- ssm_state: bfloat16 [256, 128, 64, 128], P(('groups', 'replica'), 'tensor'), parts along dimension 0, may hold values from -6 to 6
- tail_inner: bfloat16 [256, 3, 8192], P(('groups', 'replica'), None, 'tensor'), parts along dimension 0, may hold values from -6 to 6
- tail_groups: bfloat16 [256, 3, 2, 512], P(('groups', 'replica'), None, None, 'tensor'), parts along dimension 0, may hold values from -6 to 6
- key_cache: bfloat16 [256, 4, 256, 128], P(('groups', 'replica'), 'tensor'), parts along dimension 0, may hold values from -6 to 6
- value_cache: bfloat16 [256, 4, 256, 128], P(('groups', 'replica'), 'tensor'), parts along dimension 0, may hold values from -6 to 6
- cache_length: int32 [256], P('groups'), parts along dimension 0, may hold values from 32 to 256, as said below
- finished: int32 [256], P('groups'), parts along dimension 0, may hold values from 0 to 1, as said below
- source: int32 [256], P(('groups', 'replica')), parts along dimension 0, may hold values from 0 to 127, as said below
- new_inner: bfloat16 [256, 4, 8192], P(('groups', 'replica'), None, 'tensor'), parts along dimension 0, may hold values from -6 to 6
- new_gate: bfloat16 [256, 4, 8192], P(('groups', 'replica'), None, 'tensor'), parts along dimension 0, may hold values from -6 to 6
- new_groups: bfloat16 [256, 4, 2, 512], P(('groups', 'replica'), None, None, 'tensor'), parts along dimension 0, may hold values from -6 to 6
- new_delta: bfloat16 [256, 4, 128], P(('groups', 'replica'), None, 'tensor'), parts along dimension 0, may hold values from -4 to 4
- new_query: bfloat16 [256, 4, 4096], P(('groups', 'replica'), None, 'tensor'), parts along dimension 0, may hold values from -8 to 8
- new_entries: bfloat16 [256, 4, 2, 512], P(('groups', 'replica'), None, None, 'tensor'), parts along dimension 0, may hold values from -8 to 8
- filter_inner: float32 [4, 8192], P(None, 'tensor'), may hold values from -3 to 3
- filter_groups: float32 [4, 2, 512], P(None, None, 'tensor'), may hold values from -3 to 3
- decay_rate: float32 [128], P('tensor'), may hold values from 0.02 to 1
- delta_bias: float32 [128], P('tensor'), may hold values from -1.5 to 0.5
- skip_gain: float32 [128], P('tensor'), may hold values from 0.5 to 1.5
- norm_gain: float32 [8192], P('tensor'), may hold values from 0.1 to 1.9
Outputs:
- mixer_output: bfloat16 [256, 4, 8192], P(('groups', 'replica'), None, 'tensor'), parts along dimension 0
- attention_output: bfloat16 [256, 4, 4096], P(('groups', 'replica'), None, 'tensor'), parts along dimension 0
There are 2 independent parts, one for each index of `groups`. A program takes and returns all parts, laid end to end along the dimension named above; an argument that names none is the same for every part. Nothing has to cross between parts.
Inputs may be any that keep to these rules, and one draw needn't show every extreme that they name: source is a permutation of the 128 slots of a group; a rollout that stays on its replica keeps its slot; each replica hands exactly 7 rollouts to other replicas and takes exactly 7 from them, at most one between any two replicas. finished is 0 for every rollout that changes replica. `cache_length`: some entry equals 256 in every draw.
All inputs are finite; a program needn't handle non-finite values.
Results may differ from a plain program's by a relative error of at most 0.0049.
Values may be sent and summed in bfloat16 or wider, within the bound.
A program may use at most 192 MiB of HBM per device.

v0:
```python
import math

import jax
import jax.numpy as jnp
from jax import lax
from jax.sharding import PartitionSpec as P


def filtered(history, recent, weights):
    window = jnp.concatenate([history, recent], axis=1).astype(jnp.float32)
    length = recent.shape[1]
    summed = weights[0] * window[:, 0:length]
    for offset in range(1, weights.shape[0]):
        summed = summed + weights[offset] * window[:, offset : offset + length]
    return jax.nn.silu(summed)


def mixer(
    ssm_prior,
    history_inner,
    history_groups,
    new_inner,
    new_gate,
    new_groups,
    new_delta,
    filter_inner,
    filter_groups,
    decay_rate,
    delta_bias,
    skip_gain,
    norm_gain,
):
    batch_size, step_count, inner_width = new_inner.shape
    head_count, head_size, state_width = (
        ssm_prior.shape[1],
        ssm_prior.shape[2],
        ssm_prior.shape[3],
    )
    group_count = new_groups.shape[3] // state_width
    inputs = filtered(history_inner, new_inner, filter_inner).reshape(
        batch_size, step_count, head_count, head_size
    )
    mixing = filtered(history_groups, new_groups, filter_groups).reshape(
        batch_size, step_count, 2, group_count, 1, state_width
    )
    mixing = jnp.broadcast_to(
        mixing, (batch_size, step_count, 2, group_count, head_count // group_count, state_width)
    )
    mixing = mixing.reshape(batch_size, step_count, 2, head_count, state_width)
    timestep = jax.nn.softplus(new_delta.astype(jnp.float32) + delta_bias)
    retention = jnp.exp(-decay_rate * timestep)
    carried = ssm_prior.astype(jnp.float32)
    results = []
    for position in range(step_count):
        injected = (timestep[:, position, :, None] * inputs[:, position])[..., None] * mixing[
            :, position, 0, :, None, :
        ]
        carried = retention[:, position, :, None, None] * carried + injected
        readout = jnp.einsum(
            "bhpn,bhn->bhp", carried, mixing[:, position, 1], precision=lax.Precision.HIGHEST
        )
        results.append(readout + skip_gain[:, None] * inputs[:, position])
    combined = jnp.stack(results, axis=1).reshape(batch_size, step_count, inner_width)
    gated_rows = combined * jax.nn.silu(new_gate.astype(jnp.float32))
    grouped = gated_rows.reshape(batch_size, step_count, group_count, inner_width // group_count)
    inverse_rms = lax.rsqrt(jnp.mean(grouped * grouped, axis=-1, keepdims=True) + 1e-05)
    return (grouped * inverse_rms).reshape(batch_size, step_count, inner_width) * norm_gain


def attention(queries, recent, key_cache, value_cache, lengths):
    batch_size, step_count = (queries.shape[0], queries.shape[1])
    shared_heads, cache_span, head_size = (
        key_cache.shape[1],
        key_cache.shape[2],
        key_cache.shape[3],
    )
    grouped = queries.reshape(batch_size, step_count, shared_heads, -1, head_size)
    entries = recent.reshape(batch_size, step_count, 2, shared_heads, head_size)
    factor = 1.0 / math.sqrt(head_size)
    cached_scores = (
        jnp.einsum("bsjgd,bjld->bjsgl", grouped, key_cache, preferred_element_type=jnp.float32)
        * factor
    )
    recent_scores = (
        jnp.einsum(
            "bsjgd,btjd->bjsgt", grouped, entries[:, :, 0], preferred_element_type=jnp.float32
        )
        * factor
    )
    visible = jnp.arange(cache_span)[None, :] < lengths[:, None]
    cached_scores = jnp.where(visible[:, None, None, None, :], cached_scores, -jnp.inf)
    causal = jnp.arange(step_count)[None, :] <= jnp.arange(step_count)[:, None]
    recent_scores = jnp.where(causal[None, None, :, None, :], recent_scores, -jnp.inf)
    highest = jnp.maximum(jnp.max(cached_scores, axis=-1), jnp.max(recent_scores, axis=-1))[
        ..., None
    ]
    cached_weight = jnp.exp(cached_scores - highest)
    recent_weight = jnp.exp(recent_scores - highest)
    denominator = jnp.sum(cached_weight, axis=-1, keepdims=True) + jnp.sum(
        recent_weight, axis=-1, keepdims=True
    )
    cached_prob = (cached_weight / denominator).astype(jnp.bfloat16)
    recent_prob = (recent_weight / denominator).astype(jnp.bfloat16)
    attended = jnp.einsum(
        "bjsgl,bjld->bsjgd", cached_prob, value_cache, preferred_element_type=jnp.float32
    )
    attended = attended + jnp.einsum(
        "bjsgt,btjd->bsjgd", recent_prob, entries[:, :, 1], preferred_element_type=jnp.float32
    )
    return attended.reshape(batch_size, step_count, -1)


def silence(values, finished_rows):
    return (values * (1 - finished_rows).astype(jnp.float32)[:, None, None]).astype(jnp.bfloat16)


def relocate(local_rows, arrived_rows, index):
    return jnp.take(jnp.concatenate([local_rows, arrived_rows], axis=0), index, axis=0)


def body(
    ssm_state,
    tail_inner,
    tail_groups,
    key_cache,
    value_cache,
    cache_length,
    finished,
    source,
    new_inner,
    new_gate,
    new_groups,
    new_delta,
    new_query,
    new_entries,
    filter_inner,
    filter_groups,
    decay_rate,
    delta_bias,
    skip_gain,
    norm_gain,
):
    replicas = lax.axis_size("replica")
    ordinal = lax.axis_index("replica")
    per_device = ssm_state.shape[0]
    peer_ids = jnp.arange(replicas, dtype=jnp.int32)
    everywhere = lax.all_gather(source, "replica", axis=0, tiled=True).reshape(replicas, per_device)
    sends = (everywhere // per_device == ordinal) & (peer_ids[:, None] != ordinal)
    outgoing = jnp.sum(jnp.where(sends, everywhere % per_device, 0), axis=1)
    from_replica = source // per_device
    staying = from_replica == ordinal
    pick_new = jnp.where(staying, source % per_device, per_device + from_replica)
    sent_state = jnp.take(ssm_state, outgoing, axis=0)
    sent_inner = jnp.take(tail_inner, outgoing, axis=0)
    sent_groups = jnp.take(tail_groups, outgoing, axis=0)
    sent_keys = jnp.take(key_cache, outgoing, axis=0)
    sent_values = jnp.take(value_cache, outgoing, axis=0)
    arrived = (
        lax.all_to_all(sent_state, "replica", split_axis=0, concat_axis=0, tiled=True),
        lax.all_to_all(sent_inner, "replica", split_axis=0, concat_axis=0, tiled=True),
        lax.all_to_all(sent_groups, "replica", split_axis=0, concat_axis=0, tiled=True),
        lax.all_to_all(sent_keys, "replica", split_axis=0, concat_axis=0, tiled=True),
        lax.all_to_all(sent_values, "replica", split_axis=0, concat_axis=0, tiled=True),
    )
    finished_rows = jnp.take(finished, source, axis=0)
    lengths = jnp.take(cache_length, source, axis=0)
    combined = mixer(
        relocate(ssm_state, arrived[0], pick_new),
        relocate(tail_inner, arrived[1], pick_new),
        relocate(tail_groups, arrived[2], pick_new),
        new_inner,
        new_gate,
        new_groups,
        new_delta,
        filter_inner,
        filter_groups,
        decay_rate,
        delta_bias,
        skip_gain,
        norm_gain,
    )
    mixer_output = silence(combined, finished_rows)
    attended = attention(
        new_query,
        new_entries,
        relocate(key_cache, arrived[3], pick_new),
        relocate(value_cache, arrived[4], pick_new),
        lengths,
    )
    attention_output = silence(attended, finished_rows)
    return (mixer_output, attention_output)


def solution(mesh):
    in_specs = (
        P(("groups", "replica"), "tensor", None, None),
        P(("groups", "replica"), None, "tensor"),
        P(("groups", "replica"), None, None, "tensor"),
        P(("groups", "replica"), "tensor", None, None),
        P(("groups", "replica"), "tensor", None, None),
        P("groups"),
        P("groups"),
        P(("groups", "replica")),
        P(("groups", "replica"), None, "tensor"),
        P(("groups", "replica"), None, "tensor"),
        P(("groups", "replica"), None, None, "tensor"),
        P(("groups", "replica"), None, "tensor"),
        P(("groups", "replica"), None, "tensor"),
        P(("groups", "replica"), None, None, "tensor"),
        P(None, "tensor"),
        P(None, None, "tensor"),
        P("tensor"),
        P("tensor"),
        P("tensor"),
        P("tensor"),
    )
    out_specs = (P(("groups", "replica"), None, "tensor"), P(("groups", "replica"), None, "tensor"))
    return jax.shard_map(body, mesh=mesh, in_specs=in_specs, out_specs=out_specs, check_vma=False)
```

profile of v0, /device:TPU:0, one launch (start us, length us, event | category | flops | bytes accessed | tf_op | source)
XLA Modules:
  0.0 608.4 jit_solution(5231276504701128571)
XLA Ops:
  3.4 13.1 %all-reduce = s32[128]{0:T(128)S(1)} all-reduce(s32[128]{0:T(128)S(1)} %dynamic-update-slice), channel_id=1, replica_groups=mesh['groups'=2,'replica'=8,'tensor'=2] {'replica'}, use_global_device_ids=true, to_apply=%add | all-reduce | flops 128 | bytes 1024
  18.9 3.3 all-to-all-start.2
  22.2 2.1 gather_fusion.2
  25.3 3.5 all-to-all-done.2
  28.8 3.4 all-to-all-start.1
  32.3 2.3 gather_fusion.10
  34.6 2.3 gather_fusion.7
  38.2 2.2 all-to-all-done.1
  40.4 25.1 %all_to_all.25 = bf16[8,2,256,128]{3,2,1,0:T(8,128)(2,1)} all-to-all(bf16[8,2,256,128]{3,2,1,0:T(8,128)(2,1)S(1)} %get-tuple-element.50), channel_id=1, replica_groups=mesh['groups'=2,'replica'=8,'tensor'=2] {'replica'}, dimensions={0} | all-to-all | bytes 2097152 | tf_op jit(solution)/shard_map/all_to_all | solution.py:163
  65.5 3.6 all-to-all-start.4
  69.1 10.5 %gather_fusion = bf16[8,64,64,128]{3,2,1,0:T(8,128)(2,1)} fusion(bf16[16,64,64,128]{3,2,1,0:T(8,128)(2,1)} %param.26, s32[1024]{0:T(1024)S(1)} %pad_clamp_fusion.3), kind=kCustom, calls=%fused_computation.6 | custom fusion | bytes 16777248 | tf_op jit(solution)/shard_map/jit(_take)/gather | solution.py:153
  79.6 7.6 %broadcast_select_fusion.1 = bf16[8,64,64,128]{3,2,1,0:T(8,128)(2,1)} fusion(bf16[8,64,64,128]{3,2,1,0:T(8,128)(2,1)} %gather_fusion, pred[8]{0:T(512)(128)(4,1)S(1)} %compare_and_fusion.1), kind=kLoop, calls=%fused_computation.54 | loop fusion | flops 4194304 | bytes 16777224 | tf_op jit(solution)/shard_map/jit(_take)/select_n | solution.py:153
  87.2 6.1 %all-to-all-done.4 = bf16[8,2,256,128]{3,2,1,0:T(8,128)(2,1)S(1)} async-done(((bf16[8,2,256,128]{3,2,1,0:T(8,128)(2,1)}), bf16[8,2,256,128]{3,2,1,0:T(8,128)(2,1)S(1)}, u32[]{:S(2)}, u32[]{:S(2)}) %all-to-all-start.4) | async-done | bytes 1048608 | tf_op jit(solution)/shard_map/all_to_all | solution.py:162
  93.3 5.1 all-to-all-start
  107.7 2.6 fusion.98
  110.3 1.7 fusion.94
  115.5 2.1 fusion.92
  121.8 2.2 fusion.71
  124.0 3.8 pad_maximum_fusion.1
  127.9 4.0 gather_fusion.8
  131.9 3.8 pad_maximum_fusion.2
  135.7 4.0 gather_fusion.11
  139.8 2.6 fusion.97
  143.1 2.3 fusion.55
  147.0 133.1 %all-to-all-done = bf16[8,64,64,128]{3,2,1,0:T(8,128)(2,1)} async-done(((bf16[8,64,64,128]{3,2,1,0:T(8,128)(2,1)}), bf16[8,64,64,128]{3,2,1,0:T(8,128)(2,1)}, u32[]{:S(2)}, u32[]{:S(2)}) %all-to-all-start) | async-done | bytes 8388640 | tf_op jit(solution)/shard_map/all_to_all | solution.py:159
  280.1 17.5 %pad_maximum_fusion = bf16[24,64,64,128]{3,2,1,0:T(8,128)(2,1)} fusion(bf16[8,64,64,128]{3,2,1,0:T(8,128)(2,1)} %all-to-all-done, bf16[16,64,64,128]{3,2,1,0:T(8,128)(2,1)} %param.26), kind=kLoop, calls=%fused_computation.21 | loop fusion | flops 12582912 | bytes 50331648 | tf_op jit(solution)/shard_map/concatenate | solution.py:118
  297.7 15.7 %gather_fusion.1 = bf16[16,64,64,128]{3,2,1,0:T(8,128)(2,1)} fusion(bf16[24,64,64,128]{3,2,1,0:T(8,128)(2,1)} %pad_maximum_fusion, s32[1024]{0:T(1024)S(1)} %pad_clamp_fusion.2), kind=kCustom, calls=%fused_computation.7 | custom fusion | bytes 33554496 | tf_op jit(solution)/shard_map/jit(_take)/gather | solution.py:118
  313.5 59.0 %fusion.4 = f32[16,64,1,64]{3,2,1,0:T(1,128)S(1)} fusion(f32[16,64,128,1]{2,3,1,0:T(1,128)S(1)} %bitcast.150, f32[16,64,128]{2,1,0:T(8,128)S(1)} %copy-done.12, f32[16,64,64]{2,1,0:T(8,128)S(1)} %get-tuple-element.23, f32[16,64]{1,0:T(8,128)S(1)} %bitcast.163, bf16[16,64,64,128]{3,2,1,0:T(8,128)(2,1)} %gather_fusion.1, pred[16]{0:T(512)(128)(4,1)S(1)} %copy-done.36), kind=kOutput, calls=%fused_computation.19 | convolution fusion | flops 142606336 | bytes 18354192 | tf_op jit(solution)/shard_map/bhpn,bhn->bhp/dot_general | solution.py:59
  372.5 66.3 %fusion.5 = f32[16,64,1,64]{3,2,1,0:T(1,128)S(1)} fusion(f32[16,64,128,1]{2,3,1,0:T(1,128)S(1)} %bitcast.149, f32[16,64,128]{2,1,0:T(8,128)S(1)} %copy-done.11, f32[16,64,64]{2,1,0:T(8,128)S(1)} %copy-done.18, f32[16,64]{1,0:T(8,128)S(1)} %bitcast.170, f32[16,64,128]{2,1,0:T(8,128)S(1)} %copy-done.12, f32[16,64,64]{2,1,0:T(8,128)S(1)} %get-tuple-element.23, ...), kind=kOutput, calls=%fused_computation.20 | convolution fusion | flops 167772160 | bytes 19144720 | tf_op jit(solution)/shard_map/bhpn,bhn->bhp/dot_general | solution.py:59
  438.9 75.6 %fusion.6 = f32[16,64,1,64]{3,2,1,0:T(1,128)S(1)} fusion(f32[16,64,128,1]{2,3,1,0:T(1,128)S(1)} %bitcast.148, f32[16,64,128]{2,1,0:T(8,128)S(1)} %copy-done.10, f32[16,64,64]{2,1,0:T(8,128)S(1)} %copy-done.17, f32[16,64]{1,0:T(8,128)S(1)} %bitcast.168, f32[16,64,128]{2,1,0:T(8,128)S(1)} %copy-done.11, f32[16,64,64]{2,1,0:T(8,128)S(1)} %copy-done.18, ...), kind=kOutput, calls=%fused_computation.22 | convolution fusion | flops 192937984 | bytes 19935248 | tf_op jit(solution)/shard_map/bhpn,bhn->bhp/dot_general | solution.py:59
  514.5 85.6 %fusion = f32[16,64,1,64]{3,2,1,0:T(1,128)S(1)} fusion(f32[16,64,128,1]{2,3,1,0:T(1,128)S(1)} %bitcast.147, f32[16,64,128]{2,1,0:T(8,128)S(1)} %copy-done.9, f32[16,64,64]{2,1,0:T(8,128)S(1)} %get-tuple-element.24, f32[16,64]{1,0:T(8,128)S(1)} %bitcast.167, f32[16,64,128]{2,1,0:T(8,128)S(1)} %copy-done.10, f32[16,64,64]{2,1,0:T(8,128)S(1)} %copy-done.17, ...), kind=kOutput, calls=%fused_computation.12 | convolution fusion | flops 218103808 | bytes 20725776 | tf_op jit(solution)/shard_map/bhpn,bhn->bhp/dot_general | solution.py:59
  605.4 1.6 multiply_convert_fusion
  (150 shorter events, 32.2 us)
Async XLA Ops:
  0.6 99.9 %copy-start = (s32[128]{0:T(128)S(1)}, s32[128]{0:T(128)}, u32[]{:S(2)}) copy-start(s32[128]{0:T(128)} %param.31) | copy-start | bytes 1540
  18.9 9.9 %all-to-all-start.2 = ((bf16[8,3,2,256]{3,2,1,0:T(2,128)(2,1)}), bf16[8,3,2,256]{3,2,1,0:T(2,128)(2,1)S(1)}, u32[]{:S(2)}, u32[]{:S(2)}) async-start(bf16[8,3,2,256]{3,2,1,0:T(2,128)(2,1)} %broadcast_select_fusion.7), calls=%async_computation.2 | async-start | bytes 49152 | tf_op jit(solution)/shard_map/all_to_all | solution.py:161
  28.8 11.6 %all-to-all-start.1 = ((bf16[8,3,4096]{2,1,0:T(4,128)(2,1)}), bf16[8,3,4096]{2,1,0:T(4,128)(2,1)S(1)}, u32[]{:S(2)}, u32[]{:S(2)}) async-start(bf16[8,3,4096]{2,1,0:T(4,128)(2,1)} %copy.42), calls=%async_computation.1 | async-start | bytes 524288 | tf_op jit(solution)/shard_map/all_to_all | solution.py:160
  65.5 27.9 %all-to-all-start.4 = ((bf16[8,2,256,128]{3,2,1,0:T(8,128)(2,1)}), bf16[8,2,256,128]{3,2,1,0:T(8,128)(2,1)S(1)}, u32[]{:S(2)}, u32[]{:S(2)}) async-start(bf16[8,2,256,128]{3,2,1,0:T(8,128)(2,1)} %get-tuple-element.49), calls=%async_computation.4 | async-start | bytes 2097152 | tf_op jit(solution)/shard_map/all_to_all | solution.py:162
  79.6 18.9 %copy-start.6 = (bf16[16,3,4096]{2,0,1:T(8,128)(2,1)S(1)}, bf16[16,3,4096]{2,0,1:T(8,128)(2,1)}, u32[]{:S(2)}) copy-start(bf16[16,3,4096]{2,0,1:T(8,128)(2,1)} %param.27) | copy-start | bytes 1179652
  79.6 19.3 %copy-start.16 = (bf16[16,4,4096]{2,1,0:T(4,128)(2,1)S(1)}, bf16[16,4,4096]{2,1,0:T(4,128)(2,1)}, u32[]{:S(2)}) copy-start(bf16[16,4,4096]{2,1,0:T(4,128)(2,1)} %param.34) | copy-start | bytes 1572868
  79.6 21.6 %copy-start.2 = (s32[128]{0:T(128)S(1)}, s32[128]{0:T(128)}, u32[]{:S(2)}) copy-start(s32[128]{0:T(128)} %param.32) | copy-start | bytes 1540
  79.6 22.2 %copy-start.20 = (bf16[16,4,2048]{2,1,0:T(4,128)(2,1)S(1)}, bf16[16,4,2048]{2,1,0:T(4,128)(2,1)}, u32[]{:S(2)}) copy-start(bf16[16,4,2048]{2,1,0:T(4,128)(2,1)} %param.38) | copy-start | bytes 786436
  79.6 26.0 %copy-start.34 = (f32[4,2,256]{2,1,0:T(2,128)S(1)}, f32[4,2,256]{2,1,0:T(2,128)}, u32[]{:S(2)}) copy-start(f32[4,2,256]{2,1,0:T(2,128)} %param.41) | copy-start | bytes 24580
  93.3 24.2 %copy-start.7 = (bf16[8,2,256,128]{3,2,1,0:T(8,128)(2,1)}, bf16[8,2,256,128]{3,2,1,0:T(8,128)(2,1)S(1)}, u32[]{:S(2)}) copy-start(bf16[8,2,256,128]{3,2,1,0:T(8,128)(2,1)S(1)} %all-to-all-done.4) | copy-start | bytes 3145732
  93.3 186.8 %all-to-all-start = ((bf16[8,64,64,128]{3,2,1,0:T(8,128)(2,1)}), bf16[8,64,64,128]{3,2,1,0:T(8,128)(2,1)}, u32[]{:S(2)}, u32[]{:S(2)}) async-start(bf16[8,64,64,128]{3,2,1,0:T(8,128)(2,1)} %broadcast_select_fusion.1), calls=%async_computation | async-start | bytes 16777216 | tf_op jit(solution)/shard_map/all_to_all | solution.py:159
  120.5 19.3 %copy-start.36 = (pred[16]{0:T(512)(128)(4,1)S(1)}, pred[16]{0:T(512)(128)(4,1)}, u32[]{:S(2)}) copy-start(pred[16]{0:T(512)(128)(4,1)} %copy-done.35) | copy-start | bytes 52
  120.5 19.3 %copy-start.38 = (pred[16,256]{1,0:T(8,128)(4,1)S(1)}, pred[16,256]{1,0:T(8,128)(4,1)}, u32[]{:S(2)}) copy-start(pred[16,256]{1,0:T(8,128)(4,1)} %iota_compare_fusion) | copy-start | bytes 12292
  120.9 21.4 %copy-start.23 = (f32[16,2,4,8]{3,2,1,0:T(4,128)S(1)}, f32[16,2,4,8]{3,2,1,0:T(4,128)}, u32[]{:S(2)}) copy-start(f32[16,2,4,8]{3,2,1,0:T(4,128)} %get-tuple-element.53) | copy-start | bytes 12292
  121.0 21.4 %copy-start.19 = (f32[16,2,4,8,4]{3,4,2,1,0:T(4,128)S(1)}, f32[16,2,4,8,4]{3,4,2,1,0:T(4,128)}, u32[]{:S(2)}) copy-start(f32[16,2,4,8,4]{3,4,2,1,0:T(4,128)} %get-tuple-element.54) | copy-start | bytes 49156
  121.8 23.6 %copy-start.3 = (f32[16,4,64,64]{3,2,0,1:T(8,128)}, f32[16,4,64,64]{3,2,0,1:T(8,128)S(1)}, u32[]{:S(2)}) copy-start(f32[16,4,64,64]{3,2,0,1:T(8,128)S(1)} %reshape.174) | copy-start | bytes 3145732
  127.9 18.1 %copy-start.37 = (f32[16]{0:T(128)S(1)}, f32[16]{0:T(128)}, u32[]{:S(2)}) copy-start(f32[16]{0:T(128)} %get-tuple-element.48) | copy-start | bytes 196
  313.4 59.0 %copy-start.5 = (bf16[16,64,64,128]{3,2,1,0:T(8,128)(2,1)S(1)}, bf16[16,64,64,128]{3,2,1,0:T(8,128)(2,1)}, u32[]{:S(2)}) copy-start(bf16[16,64,64,128]{3,2,1,0:T(8,128)(2,1)} %gather_fusion.1) | copy-start | bytes 50331652
  313.4 59.0 %copy-start.11 = (f32[16,64,128]{2,1,0:T(8,128)S(1)}, f32[16,64,128]{2,1,0:T(8,128)}, u32[]{:S(2)}) copy-start(f32[16,64,128]{2,1,0:T(8,128)} %get-tuple-element.17) | copy-start | bytes 1572868
  313.4 59.0 %copy-start.14 = (f32[16,1,1,64,128]{4,3,0,2,1:T(8,128)S(1)}, f32[16,1,1,64,128]{4,3,0,2,1:T(8,128)}, u32[]{:S(2)}) copy-start(f32[16,1,1,64,128]{4,3,0,2,1:T(8,128)} %get-tuple-element.16) | copy-start | bytes 1572868
  313.4 59.0 %copy-start.18 = (f32[16,64,64]{2,1,0:T(8,128)S(1)}, f32[16,64,64]{2,1,0:T(8,128)}, u32[]{:S(2)}) copy-start(f32[16,64,64]{2,1,0:T(8,128)} %get-tuple-element.26) | copy-start | bytes 786436
  313.5 59.0 %copy-start.33 = (f32[16,1,64]{2,1,0:T(1,128)S(1)}, f32[16,1,64]{2,1,0:T(1,128)}, u32[]{:S(2)}) copy-start(f32[16,1,64]{2,1,0:T(1,128)} %get-tuple-element.36) | copy-start | bytes 12292
  372.5 66.3 %copy-start.10 = (f32[16,64,128]{2,1,0:T(8,128)S(1)}, f32[16,64,128]{2,1,0:T(8,128)}, u32[]{:S(2)}) copy-start(f32[16,64,128]{2,1,0:T(8,128)} %get-tuple-element.15) | copy-start | bytes 1572868
  372.5 66.3 %copy-start.13 = (f32[16,1,1,64,128]{4,3,0,2,1:T(8,128)S(1)}, f32[16,1,1,64,128]{4,3,0,2,1:T(8,128)}, u32[]{:S(2)}) copy-start(f32[16,1,1,64,128]{4,3,0,2,1:T(8,128)} %get-tuple-element.14) | copy-start | bytes 1572868
  372.5 66.3 %copy-start.17 = (f32[16,64,64]{2,1,0:T(8,128)S(1)}, f32[16,64,64]{2,1,0:T(8,128)}, u32[]{:S(2)}) copy-start(f32[16,64,64]{2,1,0:T(8,128)} %get-tuple-element.25) | copy-start | bytes 786436
  372.5 66.3 %copy-start.32 = (f32[16,1,64]{2,1,0:T(1,128)S(1)}, f32[16,1,64]{2,1,0:T(1,128)}, u32[]{:S(2)}) copy-start(f32[16,1,64]{2,1,0:T(1,128)} %get-tuple-element.35) | copy-start | bytes 12292
  438.9 75.6 %copy-start.8 = (f32[16,1,1,64,128]{4,3,0,2,1:T(8,128)S(1)}, f32[16,1,1,64,128]{4,3,0,2,1:T(8,128)}, u32[]{:S(2)}) copy-start(f32[16,1,1,64,128]{4,3,0,2,1:T(8,128)} %get-tuple-element.12) | copy-start | bytes 1572868
  438.9 75.6 %copy-start.9 = (f32[16,64,128]{2,1,0:T(8,128)S(1)}, f32[16,64,128]{2,1,0:T(8,128)}, u32[]{:S(2)}) copy-start(f32[16,64,128]{2,1,0:T(8,128)} %get-tuple-element.13) | copy-start | bytes 1572868
  438.9 75.6 %copy-start.31 = (f32[16,1,64]{2,1,0:T(1,128)S(1)}, f32[16,1,64]{2,1,0:T(1,128)}, u32[]{:S(2)}) copy-start(f32[16,1,64]{2,1,0:T(1,128)} %get-tuple-element.34) | copy-start | bytes 12292
  514.5 85.6 %copy-start.4 = (f32[16,4,64,64]{3,2,0,1:T(8,128)S(1)}, f32[16,4,64,64]{3,2,0,1:T(8,128)}, u32[]{:S(2)}) copy-start(f32[16,4,64,64]{3,2,0,1:T(8,128)} %copy-done.3) | copy-start | bytes 3145732
  514.5 85.6 %copy-start.39 = (f32[64]{0:T(128)S(1)}, f32[64]{0:T(128)}, u32[]{:S(2)}) copy-start(f32[64]{0:T(128)} %param.44) | copy-start | bytes 772
  514.5 93.7 %copy-start.1 = (s32[128]{0:T(128)S(1)}, s32[128]{0:T(128)}, u32[]{:S(2)}) copy-start(s32[128]{0:T(128)} %param.31) | copy-start | bytes 1540
  (12 other events, 124.8 us)
where the time goes:
time: 614 us; the launch traced here: 608 us
  matrix products  294 us (48%)
  waiting for transfers between devices  145 us (24%)
  local copies, waits for them, and re-layouts  62.2 us (10%)
  other arithmetic  51.1 us (8%)
  blocking collectives  38.1 us (6%)
  starting transfers between devices  15.5 us (3%)
    dot_general x4, matrix products, mixer(): jnp.einsum('bhpn,bhn->bhp', carried, mixing[:, position, 1], precision=la...  286 us
    all_to_all x1, waiting for transfers between devices, body(): lax.all_to_all(sent_state, 'replica', split_axis=0, concat_axis=0, tiled=...  133 us
    concatenate x5, other arithmetic, relocate(): jnp.concatenate([local_rows, arrived_rows], axis=0)  26.6 us
    gather x5, local copies, waits for them, and re-layouts, relocate(): jnp.take(jnp.concatenate([local_rows, arrived_rows], axis=0), index, axis=0)  25.5 us
    all_to_all x1, blocking collectives, body(): lax.all_to_all(sent_values, 'replica', split_axis=0, concat_axis=0, tiled...  25.1 us
    unnamed x1, blocking collectives  13.1 us
  transfers between devices with their start and end apart: 4, of which 4 were waited for; matrix products, arithmetic and copies ran while one was open for 12% of the time, Pallas kernels for 0%

commit v1 on v0

v1 whole, which is shorter than its diff:
```python
import functools
import math

import jax
import jax.numpy as jnp
from jax import lax
from jax.experimental import pallas as pl
from jax.experimental.pallas import tpu as pltpu
from jax.sharding import PartitionSpec as P

F32 = jnp.float32
BF16 = jnp.bfloat16
MESH = pl.DeviceIdType.MESH
VMEM_BYTES = 48 * 1024 * 1024


def greet(n, me):
    barrier = pltpu.get_barrier_semaphore()
    for d in range(1, n):
        peer = lax.rem(me + d, n)
        pl.semaphore_signal(barrier, inc=1, device_id={"replica": peer}, device_id_type=MESH)
    pl.semaphore_wait(barrier, n - 1)


def forward_kernel(n, rows, pick_ref, packed_ref, list_ref, out_ref, lists_ref, staged, sems, send_sem, recv_sem, lsend_sem, lrecv_sem):
    me = lax.axis_index("replica")
    keep = pltpu.make_async_copy(packed_ref, out_ref.at[pl.ds(0, rows)], sems.at[0])
    keep.start()
    own = pltpu.make_async_copy(list_ref, lists_ref.at[me], sems.at[1])
    own.start()
    greet(n, me)
    copies = []
    for d in range(1, n):
        peer = lax.rem(me + d, n)
        staged[d] = packed_ref[pick_ref[peer]]
        for src, dst, ss, rs in (
            (list_ref, lists_ref.at[me], lsend_sem, lrecv_sem),
            (staged.at[d], out_ref.at[rows + me], send_sem, recv_sem),
        ):
            copy = pltpu.make_async_remote_copy(
                src_ref=src,
                dst_ref=dst,
                send_sem=ss.at[d],
                recv_sem=rs.at[d],
                device_id={"replica": peer},
                device_id_type=MESH,
            )
            copy.start()
            copies.append(copy)
    keep.wait()
    own.wait()
    for copy in copies:
        copy.wait()


def back_kernel(n, rows, wide, pick_ref, done_ref, mixer_ref, attn_ref, held, sems, send_sem, recv_sem):
    me = lax.axis_index("replica")
    greet(n, me)
    copies = []
    for d in range(1, n):
        peer = lax.rem(me + d, n)
        copy = pltpu.make_async_remote_copy(
            src_ref=done_ref.at[rows + peer],
            dst_ref=held.at[rows + me],
            send_sem=send_sem.at[d],
            recv_sem=recv_sem.at[d],
            device_id={"replica": peer},
            device_id_type=MESH,
        )
        copy.start()
        copies.append(copy)
    keep = pltpu.make_async_copy(done_ref.at[pl.ds(0, rows)], held.at[pl.ds(0, rows)], sems.at[0])
    keep.start()
    keep.wait()
    for copy in copies:
        copy.wait()
    for i in range(rows):
        row = held[pick_ref[i]]
        mixer_ref[i] = row[:, :wide]
        attn_ref[i] = row[:, wide:]


def silu(v):
    return v / (1.0 + jnp.exp(-v))


def split(v):
    high = v.astype(BF16).astype(F32)
    return high, v - high


def step_kernel(
    dims,
    from_ref, to_ref, length_ref, done_ref,
    new_ref, state_ref, ti_ref, tg_ref, key_ref, value_ref,
    fi_ref, fg_ref, rate_ref, bias_ref, skip_ref, gain_ref,
    out_ref,
    expand, wi, wg, mix, cmat, prod, coef, qs, kn, vn,
):
    T, inner, heads, p, n, groups, kv, qh, hd, offs = dims
    j = pl.program_id(0)
    half = groups * n
    @pl.when(j == 0)
    def _():
        row = lax.broadcasted_iota(jnp.int32, (heads, inner), 0)
        col = lax.broadcasted_iota(jnp.int32, (heads, inner), 1)
        expand[...] = jnp.where(col // p == row, 1.0, 0.0).astype(BF16)
        kn[...] = jnp.zeros_like(kn)
        vn[...] = jnp.zeros_like(vn)

    o_inner, o_gate, o_groups, o_delta, o_query, o_entries = offs
    K = fi_ref.shape[0]
    wg[0 : K - 1, 0:half] = tg_ref[0, :, 0, :].astype(F32)
    wg[0 : K - 1, half : 2 * half] = tg_ref[0, :, 1, :].astype(F32)
    wg[K - 1 : K - 1 + T, :] = new_ref[0, :, o_groups : o_groups + 2 * half].astype(F32)
    accB = fg_ref[0, 0:1, :] * wg[0:T, 0:half]
    accC = fg_ref[0, 1:2, :] * wg[0:T, half : 2 * half]
    for k in range(1, K):
        accB = accB + fg_ref[k, 0:1, :] * wg[k : k + T, 0:half]
        accC = accC + fg_ref[k, 1:2, :] * wg[k : k + T, half : 2 * half]
    B = silu(accB)
    C = silu(accC)
    c_high, c_low = split(C)
    cmat[0:T, :] = c_high
    cmat[T : 2 * T, :] = c_low
    cm = cmat[...].astype(BF16)
    per = inner // groups
    reads = []
    for g in range(groups):
        prior = state_ref[0, g * (heads // groups) : (g + 1) * (heads // groups)].reshape(per, n)
        r = lax.dot_general(cm[:, g * n : (g + 1) * n], prior, (((1,), (1,)), ((), ())), preferred_element_type=F32)
        reads.append(r[0:T] + r[T : 2 * T])
    v = new_ref[0, :, o_delta : o_delta + heads].astype(F32) + bias_ref[...]
    ts = jnp.maximum(v, 0.0) + jnp.log1p(jnp.exp(-jnp.abs(v)))
    a = -rate_ref[...] * ts
    tri = lax.broadcasted_iota(jnp.int32, (T, heads), 0)
    cum = jnp.zeros((T, heads), F32)
    for s in range(T):
        cum = cum + jnp.where(tri >= s, a[s : s + 1], 0.0)
    for s in range(T):
        prod[s * 8 : s * 8 + T, :] = C * B[s : s + 1]
    mrow = lax.broadcasted_iota(jnp.int32, (half, heads), 0) // n
    mcol = lax.broadcasted_iota(jnp.int32, (half, heads), 1) // (heads // groups)
    gmap = jnp.where(mrow == mcol, 1.0, 0.0)
    cb = jnp.dot(prod[...], gmap, preferred_element_type=F32, precision=lax.Precision.HIGHEST)
    for s in range(T + 1):
        if s < T:
            decay = jnp.exp(jnp.where(tri >= s, cum - cum[s : s + 1], -1e30))
            block = cb[s * 8 : s * 8 + T] * decay * ts[s : s + 1]
            block = block + jnp.where(tri == s, skip_ref[...], 0.0)
        else:
            block = jnp.exp(cum)
        high, low = split(block)
        coef[s * 8 : s * 8 + T, :] = high
        coef[s * 8 + T : s * 8 + 2 * T, :] = low
    cf = coef[...].astype(BF16)
    keep = (1 - done_ref[j]).astype(F32)
    for g in range(groups):
        lanes = slice(g * per, (g + 1) * per)
        wide = jnp.dot(cf, expand[:, lanes], preferred_element_type=F32)
        wi[0 : K - 1, :] = ti_ref[0, :, lanes].astype(F32)
        wi[K - 1 : K - 1 + T, :] = new_ref[0, :, o_inner + g * per : o_inner + (g + 1) * per].astype(F32)
        acc = fi_ref[0:1, lanes] * wi[0:T, :]
        for k in range(1, K):
            acc = acc + fi_ref[k : k + 1, lanes] * wi[k : k + T, :]
        x = silu(acc)
        y = reads[g] * (wide[T * 8 : T * 8 + T] + wide[T * 8 + T : T * 8 + 2 * T])
        for s in range(T):
            y = y + (wide[s * 8 : s * 8 + T] + wide[s * 8 + T : s * 8 + 2 * T]) * x[s : s + 1]
        gate = new_ref[0, :, o_gate + g * per : o_gate + (g + 1) * per].astype(F32)
        y = y * silu(gate)
        inv = lax.rsqrt(jnp.mean(y * y, axis=-1, keepdims=True) + 1e-05)
        out_ref[0, :, lanes] = (y * inv * gain_ref[:, lanes] * keep).astype(BF16)
    length = length_ref[j]
    span = key_ref.shape[2]
    R = qh * T
    factor = 1.0 / math.sqrt(hd)
    pos = lax.broadcasted_iota(jnp.int32, (R, span), 1)
    rr = lax.broadcasted_iota(jnp.int32, (R, 16), 0) % T
    rc = lax.broadcasted_iota(jnp.int32, (R, 16), 1)
    for h in range(kv):
        for q in range(qh):
            at = o_query + (h * qh + q) * hd
            qs[h, q * T : (q + 1) * T, :] = new_ref[0, :, at : at + hd].astype(F32)
        at = o_entries + h * hd
        kn[h, 0:T, :] = new_ref[0, :, at : at + hd].astype(F32)
        at = o_entries + (kv + h) * hd
        vn[h, 0:T, :] = new_ref[0, :, at : at + hd].astype(F32)
        query = qs[h].astype(BF16)
        nt = (((1,), (1,)), ((), ()))
        old = lax.dot_general(query, key_ref[0, h], nt, preferred_element_type=F32) * factor
        new = lax.dot_general(query, kn[h].astype(BF16), nt, preferred_element_type=F32) * factor
        old = jnp.where(pos < length, old, -1e30)
        new = jnp.where(rc <= rr, new, -1e30)
        top = jnp.maximum(jnp.max(old, axis=-1, keepdims=True), jnp.max(new, axis=-1, keepdims=True))
        old = jnp.exp(old - top)
        new = jnp.exp(new - top)
        total = jnp.sum(old, axis=-1, keepdims=True) + jnp.sum(new, axis=-1, keepdims=True)
        old = (old / total).astype(BF16)
        new = (new / total).astype(BF16)
        got = jnp.dot(old, value_ref[0, h], preferred_element_type=F32)
        got = got + jnp.dot(new, vn[h].astype(BF16), preferred_element_type=F32)
        got = got * keep
        for q in range(qh):
            at = inner + (h * qh + q) * hd
            out_ref[0, :, at : at + hd] = got[q * T : (q + 1) * T].astype(BF16)


def body(
    ssm_state, tail_inner, tail_groups, key_cache, value_cache, cache_length, finished, source,
    new_inner, new_gate, new_groups, new_delta, new_query, new_entries,
    filter_inner, filter_groups, decay_rate, delta_bias, skip_gain, norm_gain,
):
    n = lax.axis_size("replica")
    me = lax.axis_index("replica")
    rows, heads, p, width = ssm_state.shape
    T, inner = new_inner.shape[1:]
    kv, span, hd = key_cache.shape[1:]
    groups = new_groups.shape[3] // width
    qwide = new_query.shape[2]
    qh = qwide // (kv * hd)
    pieces = [
        new_inner,
        new_gate,
        new_groups.reshape(rows, T, -1),
        jnp.pad(new_delta, ((0, 0), (0, 0), (0, -heads % 128))),
        new_query,
        new_entries.reshape(rows, T, -1),
    ]
    offs, total = [], 0
    for piece in pieces:
        offs.append(total)
        total += piece.shape[2]
    packed = jnp.concatenate(pieces, axis=2)
    home = source // rows
    slots = jnp.arange(rows, dtype=jnp.int32)
    peers = jnp.arange(n, dtype=jnp.int32)
    ask = jnp.sum(jnp.where(home[None, :] == peers[:, None], slots[None, :], 0), axis=1)
    ask = jnp.where(peers == me, 0, ask)
    listed = jnp.broadcast_to(jnp.pad(source, (0, 128 - rows))[None, :], (8, 128))

    hbm = pl.BlockSpec(memory_space=pl.ANY)
    vmem = pl.BlockSpec(memory_space=pltpu.VMEM)
    smem = pl.BlockSpec(memory_space=pltpu.SMEM)
    dma = pltpu.SemaphoreType.DMA
    inputs, lists = pl.pallas_call(
        functools.partial(forward_kernel, n, rows),
        out_shape=(
            jax.ShapeDtypeStruct((rows + n, T, total), BF16),
            jax.ShapeDtypeStruct((n, 8, 128), jnp.int32),
        ),
        in_specs=[smem, vmem, vmem],
        out_specs=(hbm, hbm),
        scratch_shapes=[
            pltpu.VMEM((n, T, total), BF16),
            dma((2,)), dma((n,)), dma((n,)), dma((n,)), dma((n,)),
        ],
        compiler_params=pltpu.CompilerParams(collective_id=0, has_side_effects=True, vmem_limit_bytes=VMEM_BYTES),
    )(ask, packed, listed)

    everywhere = lists[:, 0, :rows]
    mine = (me * rows + slots)[:, None, None] == everywhere[None, :, :]
    taker = jnp.sum(jnp.where(mine, peers[None, :, None], 0), axis=(1, 2))
    place = jnp.where(taker == me, slots, rows + taker).astype(jnp.int32)
    lengths = lax.dynamic_slice_in_dim(cache_length, me * rows, rows)
    done = lax.dynamic_slice_in_dim(finished, me * rows, rows)

    dims = (T, inner, heads, p, width, groups, kv, qh, hd, tuple(offs))
    owide = inner + qwide

    def at(shape):
        zeros = (0,) * (len(shape) - 1)
        return pl.BlockSpec((1,) + shape[1:], lambda j, *_: (j,) + zeros)

    def whole(a):
        zeros = (0,) * a.ndim
        return pl.BlockSpec(a.shape, lambda j, *_: zeros)

    params = [filter_inner, filter_groups, decay_rate[None], delta_bias[None], skip_gain[None], norm_gain[None]]
    half = groups * width
    outs = pl.pallas_call(
        functools.partial(step_kernel, dims),
        out_shape=jax.ShapeDtypeStruct((rows + n, T, owide), BF16),
        grid_spec=pltpu.PrefetchScalarGridSpec(
            num_scalar_prefetch=4,
            grid=(rows,),
            in_specs=[
                pl.BlockSpec((1, T, total), lambda j, f, *_: (f[j], 0, 0)),
                at(ssm_state.shape), at(tail_inner.shape), at(tail_groups.shape),
                at(key_cache.shape), at(value_cache.shape),
            ] + [whole(a) for a in params],
            out_specs=pl.BlockSpec((1, T, owide), lambda j, f, t, *_: (t[j], 0, 0)),
            scratch_shapes=[
                pltpu.VMEM((heads, inner), BF16),
                pltpu.VMEM((8, inner // groups), F32),
                pltpu.VMEM((8, 2 * half), F32),
                pltpu.VMEM((8, 2 * half), F32),
                pltpu.VMEM((2 * T, half), F32),
                pltpu.VMEM((T * 8, half), F32),
                pltpu.VMEM((T * 8 + 8, heads), F32),
                pltpu.VMEM((kv, qh * T, hd), F32),
                pltpu.VMEM((kv, 16, hd), F32),
                pltpu.VMEM((kv, 16, hd), F32),
            ],
        ),
        compiler_params=pltpu.CompilerParams(vmem_limit_bytes=VMEM_BYTES),
    )(place, place, lengths, done, inputs, ssm_state, tail_inner, tail_groups, key_cache, value_cache, *params)

    pick = jnp.where(home == me, slots, rows + home).astype(jnp.int32)
    return pl.pallas_call(
        functools.partial(back_kernel, n, rows, inner),
        out_shape=(
            jax.ShapeDtypeStruct((rows, T, inner), BF16),
            jax.ShapeDtypeStruct((rows, T, qwide), BF16),
        ),
        in_specs=[smem, hbm],
        out_specs=(vmem, vmem),
        scratch_shapes=[
            pltpu.VMEM((rows + n, T, owide), BF16),
            dma((1,)), dma((n,)), dma((n,)),
        ],
        compiler_params=pltpu.CompilerParams(collective_id=1, has_side_effects=True, vmem_limit_bytes=VMEM_BYTES),
    )(pick, outs)


def solution(mesh):
    in_specs = (
        P(("groups", "replica"), "tensor", None, None),
        P(("groups", "replica"), None, "tensor"),
        P(("groups", "replica"), None, None, "tensor"),
        P(("groups", "replica"), "tensor", None, None),
        P(("groups", "replica"), "tensor", None, None),
        P("groups"),
        P("groups"),
        P(("groups", "replica")),
        P(("groups", "replica"), None, "tensor"),
        P(("groups", "replica"), None, "tensor"),
        P(("groups", "replica"), None, None, "tensor"),
        P(("groups", "replica"), None, "tensor"),
        P(("groups", "replica"), None, "tensor"),
        P(("groups", "replica"), None, None, "tensor"),
        P(None, "tensor"),
        P(None, None, "tensor"),
        P("tensor"),
        P("tensor"),
        P("tensor"),
        P("tensor"),
    )
    out_specs = (P(("groups", "replica"), None, "tensor"), P(("groups", "replica"), None, "tensor"))
    return jax.shard_map(body, mesh=mesh, in_specs=in_specs, out_specs=out_specs, check_vma=False)
```

time: 614 us -> 82.5 us (0.13)
  matrix products: 294 us -> 0 us
  waiting for transfers between devices: 145 us -> 0 us
  Pallas kernels: 0 us -> 59.9 us
  other arithmetic: 51.1 us -> 2.33 us
  local copies, waits for them, and re-layouts: 62.2 us -> 18.8 us
  blocking collectives: 38.1 us -> 0 us
  starting transfers between devices: 15.5 us -> 0 us
    dot_general x8 -> x0, matrix products: 294 us -> none  [the longest x4 286 us: mixer(): jnp.einsum('bhpn,bhn->bhp', carried, mixing[:, position, 1], precision=la...]
    all_to_all x4 -> x0, waiting for transfers between devices: 145 us -> none  [the longest x1 133 us: body(): lax.all_to_all(sent_state, 'replica', split_axis=0, concat_axis=0, tiled=...]
    pallas_call x0 -> x3, Pallas kernels: none -> 59.9 us  [the longest x1 24.6 us: body(): pl.pallas_call(functools.partial(step_kernel, dims), out_shape=jax.ShapeD...]
    gather x12 -> x0, local copies, waits for them, and re-layouts: 45.5 us -> none  [the longest x5 25.5 us: relocate(): jnp.take(jnp.concatenate([local_rows, arrived_rows], axis=0), index, axis=0)]
    concatenate x5 -> x0, other arithmetic: 26.6 us -> none  [relocate(): jnp.concatenate([local_rows, arrived_rows], axis=0)]
    all_to_all x1 -> x0, blocking collectives: 25.1 us -> none  [body(): lax.all_to_all(sent_values, 'replica', split_axis=0, concat_axis=0, tiled...]
    all_to_all x4 -> x0, starting transfers between devices: 15.5 us -> none  [the longest x1 5.14 us: body(): lax.all_to_all(sent_state, 'replica', split_axis=0, concat_axis=0, tiled=...]
    unnamed x1 -> x0, blocking collectives: 13.1 us -> none
  transfers between devices with their start and end apart: 4 -> 0, of which waited for: 4 -> 0; matrix products, arithmetic and copies ran while one was open for 12% -> 0% of each run, Pallas kernels for 0% -> 0%
where the time goes in v1:
time: 82.5 us; the launch traced here: 81.9 us
  Pallas kernels  59.9 us (73%)
  local copies, waits for them, and re-layouts  18.8 us (23%)
  other arithmetic  2.33 us (3%)
    pallas_call x1, Pallas kernels, body(): pl.pallas_call(functools.partial(step_kernel, dims), out_shape=jax.ShapeD...  24.6 us
    pallas_call x1, Pallas kernels, body(): pl.pallas_call(functools.partial(forward_kernel, n, rows), out_shape=(jax...  19.4 us
    pallas_call x1, Pallas kernels, body(): pl.pallas_call(functools.partial(back_kernel, n, rows, inner), out_shape=...  15.9 us
    unnamed x38, local copies, waits for them, and re-layouts  14.1 us
    reshape x1, local copies, waits for them, and re-layouts, body(): new_entries.reshape(rows, T, -1)  1.67 us

profile of v1, /device:TPU:0, one launch (start us, length us, event | category | flops | bytes accessed | tf_op | source)
XLA Modules:
  0.0 81.9 jit_solution(17124868739634180580)
XLA Ops:
  0.6 0.0 copy-start.13
  0.6 0.0 copy-start.14
  0.7 1.2 %compare_select_fusion.2 = (s32[16]{0:T(128)}, s32[16]{0:T(128)S(1)}) fusion(s32[]{:T(128)S(6)} %axis_index.15, s32[16]{0:T(128)} %param.27), kind=kLoop, calls=%fused_computation.11 | loop fusion | flops 288 | bytes 196 | tf_op jit(solution)/shard_map/jit(_where)/select_n | solution.py:309
  1.9 0.1 select_reduce_fusion.1
  2.0 0.5 compare_select_fusion.1.pick_ref
  2.5 1.2 %constant_dynamic-update-slice_fusion.4 = bf16[16,4,11392]{2,1,0:T(4,128)(2,1)S(1)} fusion(bf16[16,4,4096]{2,1,0:T(4,128)(2,1)} %param.28), kind=kLoop, calls=%fused_computation.6 | loop fusion | bytes 1048576
  3.8 1.3 %constant_dynamic-update-slice_fusion.3 = bf16[16,4,11392]{2,1,0:T(4,128)(2,1)S(1)} fusion(bf16[16,4,11392]{2,1,0:T(4,128)(2,1)S(1)} %constant_dynamic-update-slice_fusion.4, bf16[16,4,4096]{2,1,0:T(4,128)(2,1)} %param.29), kind=kLoop, calls=%fused_computation.5 | loop fusion | bytes 1048576
  5.2 0.1 constant_dynamic-update-slice_fusion.1
  5.4 0.0 copy-start.1
  5.4 1.7 %reshape.18 = bf16[16,4,512]{2,1,0:T(4,128)(2,1)} reshape(bf16[16,4,2,256]{3,2,1,0:T(2,128)(2,1)} %param.33) | data formatting | bytes 131072 | tf_op jit(solution)/shard_map/reshape | solution.py:228
  7.0 0.9 %constant_dynamic-update-slice_fusion.packed_ref = bf16[16,4,11392]{2,1,0:T(4,128)(2,1)S(1)} fusion(bf16[16,4,11392]{2,1,0:T(4,128)(2,1)S(1)} %constant_dynamic-update-slice_fusion.1, bf16[16,4,512]{2,1,0:T(4,128)(2,1)} %reshape.18), kind=kLoop, calls=%fused_computation.2 | loop fusion | bytes 131072 | tf_op jit(solution)/shard_map/concatenate | solution.py:234
  7.9 0.7 pad.9
  8.6 0.6 copy-done.11
  9.2 19.4 %shard_map.203 = (bf16[24,4,11392]{2,1,0:T(4,128)(2,1)S(1)}, s32[8,8,128]{2,1,0:T(8,128)S(1)}) custom-call(s32[8]{0:T(128)S(1)} %copy-done.11, bf16[16,4,11392]{2,1,0:T(4,128)(2,1)S(1)} %constant_dynamic-update-slice_fusion.packed_ref, s32[8,128]{1,0:T(8,128)S(1)} %broadcast_in_dim.54.list_ref), custom_call_target="tpu_custom_call" | custom-call | tf_op jit(solution)/shard_map/pallas_call | solution.py:246
  28.6 1.4 %copy-done = bf16[24,4,11392]{2,1,0:T(4,128)(2,1)} copy-done((bf16[24,4,11392]{2,1,0:T(4,128)(2,1)}, bf16[24,4,11392]{2,1,0:T(4,128)(2,1)S(1)}, u32[]{:S(2)}) %copy-start) | copy-done | bytes 2187288
  30.0 0.4 select_reduce_fusion
  30.4 0.7 dynamic_slice.6.length_ref
  31.2 0.7 dynamic_slice.7.done_ref
  31.9 1.3 %copy.23.ti_ref = bf16[16,3,4096]{2,1,0:T(4,128)(2,1)S(1)} copy(bf16[16,3,4096]{2,0,1:T(8,128)(2,1)} %param.21) | data formatting | bytes 786432 | tf_op args[1]
  33.2 0.0 copy-start.2
  33.3 1.6 %copy-done.2 = bf16[16,2,256,128]{3,2,1,0:T(8,128)(2,1)S(1)} copy-done((bf16[16,2,256,128]{3,2,1,0:T(8,128)(2,1)S(1)}, bf16[16,2,256,128]{3,2,1,0:T(8,128)(2,1)}, u32[]{:S(2)}) %copy-start.2) | copy-done | bytes 2097176
  34.8 0.8 %copy-done.3 = f32[4,4096]{1,0:T(4,128)S(1)} copy-done((f32[4,4096]{1,0:T(4,128)S(1)}, f32[4,4096]{1,0:T(4,128)}, u32[]{:S(2)}) %copy-start.3) | copy-done | bytes 65560
  35.7 0.8 copy-done.4
  36.5 0.7 copy-done.5
  37.2 0.7 copy-done.6
  37.9 0.7 copy-done.8
  38.5 0.7 copy-done.9
  39.2 0.7 copy-done.10
  39.9 24.6 %shard_map.204.done_ref = bf16[24,4,6144]{2,1,0:T(4,128)(2,1)S(1)} custom-call(s32[16]{0:T(128)S(1)} %compare_select_fusion.from_ref.to_ref, s32[16]{0:T(128)S(1)} %compare_select_fusion.from_ref.to_ref, s32[16]{0:T(128)S(1)} %dynamic_slice.6.length_ref, s32[16]{0:T(128)S(1)} %dynamic_slice.7.done_ref, bf16[24,4,11392]{2,1,0:T(4,128)(2,1)} %copy-done, ...), custom_call_target="tpu_custom_call" | custom-call | tf_op jit(solution)/shard_map/pallas_call | solution.py:281
  64.5 15.9 %shard_map.205 = (bf16[16,4,4096]{2,1,0:T(4,128)(2,1)S(1)}, bf16[16,4,2048]{2,1,0:T(4,128)(2,1)S(1)}) custom-call(s32[16]{0:T(128)S(1)} %copy-done.7, bf16[24,4,6144]{2,1,0:T(4,128)(2,1)S(1)} %shard_map.204.done_ref), custom_call_target="tpu_custom_call" | custom-call | tf_op jit(solution)/shard_map/pallas_call | solution.py:310
  80.4 0.8 copy.31
  81.2 0.7 copy.32
  (23 shorter events, 0.2 us)
Async XLA Ops:
  0.6 4.4 %copy-start.13 = (bf16[16,4,2,256]{3,2,1,0:T(2,128)(2,1)S(1)}, bf16[16,4,2,256]{3,2,1,0:T(2,128)(2,1)}, u32[]{:S(2)}) copy-start(bf16[16,4,2,256]{3,2,1,0:T(2,128)(2,1)} %param.30) | copy-start | bytes 196612
  0.6 4.5 %copy-start.14 = (bf16[16,4,64]{2,1,0:T(4,128)(2,1)S(1)}, bf16[16,4,64]{2,1,0:T(4,128)(2,1)}, u32[]{:S(2)}) copy-start(bf16[16,4,64]{2,1,0:T(4,128)(2,1)} %param.31) | copy-start | bytes 24580
  0.7 4.6 %copy-start.12 = (bf16[16,4,2048]{2,1,0:T(4,128)(2,1)S(1)}, bf16[16,4,2048]{2,1,0:T(4,128)(2,1)}, u32[]{:S(2)}) copy-start(bf16[16,4,2048]{2,1,0:T(4,128)(2,1)} %param.32) | copy-start | bytes 786436
  5.4 27.9 %copy-start.1 = (bf16[16,2,256,128]{3,2,1,0:T(8,128)(2,1)S(1)}, bf16[16,2,256,128]{3,2,1,0:T(8,128)(2,1)}, u32[]{:S(2)}) copy-start(bf16[16,2,256,128]{3,2,1,0:T(8,128)(2,1)} %key_ref.1) | copy-start | bytes 6291460
  8.6 0.6 copy-start.11
  28.6 1.4 %copy-start = (bf16[24,4,11392]{2,1,0:T(4,128)(2,1)}, bf16[24,4,11392]{2,1,0:T(4,128)(2,1)S(1)}, u32[]{:S(2)}) copy-start(bf16[24,4,11392]{2,1,0:T(4,128)(2,1)S(1)} %get-tuple-element.5.new_ref) | copy-start | bytes 6561796
  33.2 1.6 %copy-start.2 = (bf16[16,2,256,128]{3,2,1,0:T(8,128)(2,1)S(1)}, bf16[16,2,256,128]{3,2,1,0:T(8,128)(2,1)}, u32[]{:S(2)}) copy-start(bf16[16,2,256,128]{3,2,1,0:T(8,128)(2,1)} %value_ref.1) | copy-start | bytes 6291460
  34.8 0.8 %copy-start.3 = (f32[4,4096]{1,0:T(4,128)S(1)}, f32[4,4096]{1,0:T(4,128)}, u32[]{:S(2)}) copy-start(f32[4,4096]{1,0:T(4,128)} %fi_ref.1) | copy-start | bytes 196612
  35.7 0.8 copy-start.4
  36.5 0.7 copy-start.5
  37.2 0.7 copy-start.6
  37.9 0.7 copy-start.8
  38.5 0.7 copy-start.9
  39.2 0.7 copy-start.10
  39.9 24.6 %copy-start.7 = (s32[16]{0:T(128)S(1)}, s32[16]{0:T(128)}, u32[]{:S(2)}) copy-start(s32[16]{0:T(128)} %get-tuple-element.6.pick_ref) | copy-start | bytes 196

commit v2 on v1

--- a/solution.py
+++ b/solution.py
@@ -11,7 +11,8 @@
 F32 = jnp.float32
 BF16 = jnp.bfloat16
 MESH = pl.DeviceIdType.MESH
-VMEM_BYTES = 48 * 1024 * 1024
+VMEM_BYTES = 60 * 1024 * 1024
+TOGETHER = 2
 
 
 def greet(n, me):
@@ -53,14 +54,15 @@
         copy.wait()
 
 
-def back_kernel(n, rows, wide, pick_ref, done_ref, mixer_ref, attn_ref, held, sems, send_sem, recv_sem):
+def back_kernel(n, rows, wide, pick_ref, give_ref, done_ref, mixer_ref, attn_ref, held, staged, send_sem, recv_sem):
     me = lax.axis_index("replica")
     greet(n, me)
     copies = []
     for d in range(1, n):
         peer = lax.rem(me + d, n)
+        staged[d] = done_ref[give_ref[peer]]
         copy = pltpu.make_async_remote_copy(
-            src_ref=done_ref.at[rows + peer],
+            src_ref=staged.at[d],
             dst_ref=held.at[rows + me],
             send_sem=send_sem.at[d],
             recv_sem=recv_sem.at[d],
@@ -69,9 +71,8 @@
         )
         copy.start()
         copies.append(copy)
-    keep = pltpu.make_async_copy(done_ref.at[pl.ds(0, rows)], held.at[pl.ds(0, rows)], sems.at[0])
-    keep.start()
-    keep.wait()
+    for i in range(rows):
+        held[i] = done_ref[i]
     for copy in copies:
         copy.wait()
     for i in range(rows):
@@ -89,25 +90,39 @@
     return high, v - high
 
 
-def step_kernel(
-    dims,
-    from_ref, to_ref, length_ref, done_ref,
-    new_ref, state_ref, ti_ref, tg_ref, key_ref, value_ref,
-    fi_ref, fg_ref, rate_ref, bias_ref, skip_ref, gain_ref,
-    out_ref,
-    expand, wi, wg, mix, cmat, prod, coef, qs, kn, vn,
-):
+def step_kernel(dims, rows, index_ref, *refs):
     T, inner, heads, p, n, groups, kv, qh, hd, offs = dims
-    j = pl.program_id(0)
-    half = groups * n
-    @pl.when(j == 0)
+    news, refs = refs[:TOGETHER], refs[TOGETHER:]
+    slabs, params, out_ref, expand, own = refs[:5], refs[5:11], refs[11], refs[12], refs[13:]
+
+    @pl.when(pl.program_id(0) == 0)
     def _():
         row = lax.broadcasted_iota(jnp.int32, (heads, inner), 0)
         col = lax.broadcasted_iota(jnp.int32, (heads, inner), 1)
         expand[...] = jnp.where(col // p == row, 1.0, 0.0).astype(BF16)
-        kn[...] = jnp.zeros_like(kn)
-        vn[...] = jnp.zeros_like(vn)
-
+        own[-1][...] = jnp.zeros_like(own[-1])
+        own[-2][...] = jnp.zeros_like(own[-2])
+
+    count = (index_ref.shape[0] - rows - 1) // 2
+    me = index_ref[index_ref.shape[0] - 1]
+    for u in range(TOGETHER):
+        slot = me * rows + pl.program_id(0) * TOGETHER + u
+        part = [ref.at[pl.ds(u, 1)] for ref in slabs]
+        one_slot(
+            dims, index_ref[rows + slot], index_ref[rows + count + slot], news[u], *part, *params,
+            out_ref.at[pl.ds(u, 1)], expand, *[ref.at[u] for ref in own],
+        )
+
+
+def one_slot(
+    dims, length, finished_here,
+    new_ref, state_ref, ti_ref, tg_ref, key_ref, value_ref,
+    fi_ref, fg_ref, rate_ref, bias_ref, skip_ref, gain_ref,
+    out_ref,
+    expand, wi, wg, cmat, prod, coef, qs, kn, vn,
+):
+    T, inner, heads, p, n, groups, kv, qh, hd, offs = dims
+    half = groups * n
     o_inner, o_gate, o_groups, o_delta, o_query, o_entries = offs
     K = fi_ref.shape[0]
     wg[0 : K - 1, 0:half] = tg_ref[0, :, 0, :].astype(F32)
@@ -154,7 +169,7 @@
         coef[s * 8 : s * 8 + T, :] = high
         coef[s * 8 + T : s * 8 + 2 * T, :] = low
     cf = coef[...].astype(BF16)
-    keep = (1 - done_ref[j]).astype(F32)
+    keep = (1 - finished_here).astype(F32)
     for g in range(groups):
         lanes = slice(g * per, (g + 1) * per)
         wide = jnp.dot(cf, expand[:, lanes], preferred_element_type=F32)
@@ -171,7 +186,6 @@
         y = y * silu(gate)
         inv = lax.rsqrt(jnp.mean(y * y, axis=-1, keepdims=True) + 1e-05)
         out_ref[0, :, lanes] = (y * inv * gain_ref[:, lanes] * keep).astype(BF16)
-    length = length_ref[j]
     span = key_ref.shape[2]
     R = qh * T
     factor = 1.0 / math.sqrt(hd)
@@ -262,15 +276,16 @@
     mine = (me * rows + slots)[:, None, None] == everywhere[None, :, :]
     taker = jnp.sum(jnp.where(mine, peers[None, :, None], 0), axis=(1, 2))
     place = jnp.where(taker == me, slots, rows + taker).astype(jnp.int32)
-    lengths = lax.dynamic_slice_in_dim(cache_length, me * rows, rows)
-    done = lax.dynamic_slice_in_dim(finished, me * rows, rows)
+    index = jnp.concatenate([place, cache_length, finished, me.astype(jnp.int32)[None]])
+    give = jnp.sum(jnp.where(mine, slots[:, None, None], 0), axis=(0, 2)).astype(jnp.int32)
+    give = jnp.where(peers == me, 0, give)
 
     dims = (T, inner, heads, p, width, groups, kv, qh, hd, tuple(offs))
     owide = inner + qwide
 
     def at(shape):
         zeros = (0,) * (len(shape) - 1)
-        return pl.BlockSpec((1,) + shape[1:], lambda j, *_: (j,) + zeros)
+        return pl.BlockSpec((TOGETHER,) + shape[1:], lambda j, *_: (j,) + zeros)
 
     def whole(a):
         zeros = (0,) * a.ndim
@@ -279,32 +294,33 @@
     params = [filter_inner, filter_groups, decay_rate[None], delta_bias[None], skip_gain[None], norm_gain[None]]
     half = groups * width
     outs = pl.pallas_call(
-        functools.partial(step_kernel, dims),
-        out_shape=jax.ShapeDtypeStruct((rows + n, T, owide), BF16),
+        functools.partial(step_kernel, dims, rows),
+        out_shape=jax.ShapeDtypeStruct((rows, T, owide), BF16),
         grid_spec=pltpu.PrefetchScalarGridSpec(
-            num_scalar_prefetch=4,
-            grid=(rows,),
+            num_scalar_prefetch=1,
+            grid=(rows // TOGETHER,),
             in_specs=[
-                pl.BlockSpec((1, T, total), lambda j, f, *_: (f[j], 0, 0)),
+                pl.BlockSpec((1, T, total), functools.partial(lambda u, j, f: (f[j * TOGETHER + u], 0, 0), u))
+                for u in range(TOGETHER)
+            ] + [
                 at(ssm_state.shape), at(tail_inner.shape), at(tail_groups.shape),
                 at(key_cache.shape), at(value_cache.shape),
             ] + [whole(a) for a in params],
-            out_specs=pl.BlockSpec((1, T, owide), lambda j, f, t, *_: (t[j], 0, 0)),
+            out_specs=at((rows, T, owide)),
             scratch_shapes=[
                 pltpu.VMEM((heads, inner), BF16),
-                pltpu.VMEM((8, inner // groups), F32),
-                pltpu.VMEM((8, 2 * half), F32),
-                pltpu.VMEM((8, 2 * half), F32),
-                pltpu.VMEM((2 * T, half), F32),
-                pltpu.VMEM((T * 8, half), F32),
-                pltpu.VMEM((T * 8 + 8, heads), F32),
-                pltpu.VMEM((kv, qh * T, hd), F32),
-                pltpu.VMEM((kv, 16, hd), F32),
-                pltpu.VMEM((kv, 16, hd), F32),
+                pltpu.VMEM((TOGETHER, 8, inner // groups), F32),
+                pltpu.VMEM((TOGETHER, 8, 2 * half), F32),
+                pltpu.VMEM((TOGETHER, 2 * T, half), F32),
+                pltpu.VMEM((TOGETHER, T * 8, half), F32),
+                pltpu.VMEM((TOGETHER, T * 8 + 8, heads), F32),
+                pltpu.VMEM((TOGETHER, kv, qh * T, hd), F32),
+                pltpu.VMEM((TOGETHER, kv, 16, hd), F32),
+                pltpu.VMEM((TOGETHER, kv, 16, hd), F32),
             ],
         ),
         compiler_params=pltpu.CompilerParams(vmem_limit_bytes=VMEM_BYTES),
-    )(place, place, lengths, done, inputs, ssm_state, tail_inner, tail_groups, key_cache, value_cache, *params)
+    )(index, *[inputs] * TOGETHER, ssm_state, tail_inner, tail_groups, key_cache, value_cache, *params)
 
     pick = jnp.where(home == me, slots, rows + home).astype(jnp.int32)
     return pl.pallas_call(
@@ -313,14 +329,15 @@
             jax.ShapeDtypeStruct((rows, T, inner), BF16),
             jax.ShapeDtypeStruct((rows, T, qwide), BF16),
         ),
-        in_specs=[smem, hbm],
+        in_specs=[smem, smem, vmem],
         out_specs=(vmem, vmem),
         scratch_shapes=[
             pltpu.VMEM((rows + n, T, owide), BF16),
-            dma((1,)), dma((n,)), dma((n,)),
+            pltpu.VMEM((n, T, owide), BF16),
+            dma((n,)), dma((n,)),
         ],
         compiler_params=pltpu.CompilerParams(collective_id=1, has_side_effects=True, vmem_limit_bytes=VMEM_BYTES),
-    )(pick, outs)
+    )(pick, give, outs)
 
 
 def solution(mesh):

time: 82.5 us -> 77.1 us (0.935)
  local copies, waits for them, and re-layouts: 18.8 us -> 9.68 us
  Pallas kernels: 59.9 us -> 62.7 us
  other arithmetic: 2.33 us -> 3.56 us
    unnamed x38 -> x26, local copies, waits for them, and re-layouts: 14.1 us -> 8.14 us
    reshape x1, local copies, waits for them, and re-layouts: 1.67 us -> 0.05 us  [body(): new_entries.reshape(rows, T, -1)]
    pallas_call x1, Pallas kernels: 15.9 us -> 17.4 us  [body(): pl.pallas_call(functools.partial(back_kernel, n, rows, inner), out_shape=...]
    dynamic_slice x2 -> x0, local copies, waits for them, and re-layouts: 1.46 us -> none  [the longest x1 0.73 us: body(): lengths = lax.dynamic_slice_in_dim(cache_length, me * rows, rows)]
    concatenate x1, local copies, waits for them, and re-layouts: 0.87 us -> 0.03 us  [body(): packed = jnp.concatenate(pieces, axis=2)]
where the time goes in v2:
time: 77.1 us; the launch traced here: 76.7 us
  Pallas kernels  62.7 us (81%)
  local copies, waits for them, and re-layouts  9.68 us (13%)
  other arithmetic  3.56 us (5%)
  between operations  0.81 us (1%)
    pallas_call x1, Pallas kernels, body(): pl.pallas_call(functools.partial(step_kernel, dims, rows), out_shape=jax....  25.3 us
    pallas_call x1, Pallas kernels, body(): pl.pallas_call(functools.partial(forward_kernel, n, rows), out_shape=(jax...  20 us
    pallas_call x1, Pallas kernels, body(): pl.pallas_call(functools.partial(back_kernel, n, rows, inner), out_shape=...  17.4 us
    unnamed x26, local copies, waits for them, and re-layouts  8.14 us

profile of v2, /device:TPU:0, one launch (start us, length us, event | category | flops | bytes accessed | tf_op | source)
XLA Modules:
  0.0 76.7 jit_solution(8463850034320606645)
XLA Ops:
  0.6 0.0 copy-start.3
  0.6 0.0 copy-start.5
  0.7 0.0 copy-start.2
  0.7 1.2 %compare_select_fusion.3 = (s32[16]{0:T(128)}, s32[16]{0:T(128)S(1)}) fusion(s32[]{:T(128)} %axis_index.15, s32[16]{0:T(128)} %param.27), kind=kLoop, calls=%fused_computation.14 | loop fusion | flops 288 | bytes 196 | tf_op jit(solution)/shard_map/jit(_where)/select_n | solution.py:325
  1.9 0.1 select_reduce_fusion
  2.0 0.5 compare_select_fusion.8.pick_ref
  2.5 1.3 %constant_dynamic-update-slice_fusion.4 = bf16[16,4,11392]{2,1,0:T(4,128)(2,1)S(1)} fusion(bf16[16,4,4096]{2,1,0:T(4,128)(2,1)} %param.28), kind=kLoop, calls=%fused_computation.9 | loop fusion | bytes 1048576
  3.8 1.3 %constant_dynamic-update-slice_fusion.3 = bf16[16,4,11392]{2,1,0:T(4,128)(2,1)S(1)} fusion(bf16[16,4,11392]{2,1,0:T(4,128)(2,1)S(1)} %constant_dynamic-update-slice_fusion.4, bf16[16,4,4096]{2,1,0:T(4,128)(2,1)} %param.29), kind=kLoop, calls=%fused_computation.8 | loop fusion | bytes 1048576
  5.0 0.0 copy-done.3
  5.1 0.0 copy-start.7
  5.1 0.0 copy-start.8
  5.1 0.0 copy-start.1
  5.2 0.0 copy-done.5
  5.2 0.0 copy-done.2
  5.2 0.1 constant_dynamic-update-slice_fusion.1
  5.4 0.0 copy-done.4
  5.5 0.0 copy-done.6
  5.5 0.0 copy-start
  5.5 0.6 broadcast_in_dim.69.list_ref
  6.2 0.4 copy-done
  6.6 20.0 %shard_map.203 = (bf16[24,4,11392]{2,1,0:T(4,128)(2,1)}, s32[8,8,128]{2,1,0:T(8,128)}) custom-call(s32[8]{0:T(128)} %compare_select_fusion.8.pick_ref, bf16[16,4,11392]{2,1,0:T(4,128)(2,1)} %copy-done, s32[8,128]{1,0:T(8,128)} %broadcast_in_dim.69.list_ref), custom_call_target="tpu_custom_call" | custom-call | tf_op jit(solution)/shard_map/pallas_call | solution.py:260
  26.6 0.8 slice.3
  27.3 0.5 fusion.1
  27.8 0.6 compare_select_fusion.7.give_ref
  28.4 0.0 copy-done.7
  28.4 0.7 pad_add_fusion.index_ref
  29.1 0.0 copy-done.1
  29.1 1.1 %copy.23.refs_3_ = bf16[16,3,4096]{2,1,0:T(4,128)(2,1)} copy(bf16[16,3,4096]{2,0,1:T(8,128)(2,1)S(1)} %copy-done.1) | data formatting | bytes 786432 | tf_op args[1]
  30.2 25.3 %shard_map.204.done_ref = bf16[16,4,6144]{2,1,0:T(4,128)(2,1)} custom-call(s32[273]{0:T(512)} %pad_add_fusion.index_ref, bf16[24,4,11392]{2,1,0:T(4,128)(2,1)} %get-tuple-element.5.refs_0_.refs_1_, bf16[24,4,11392]{2,1,0:T(4,128)(2,1)} %get-tuple-element.5.refs_0_.refs_1_, bf16[16,64,64,128]{3,2,1,0:T(8,128)(2,1)} %refs_2_.1, ...), custom_call_target="tpu_custom_call" | custom-call | tf_op jit(solution)/shard_map/pallas_call | solution.py:296
  55.5 17.4 %shard_map.205 = (bf16[16,4,4096]{2,1,0:T(4,128)(2,1)}, bf16[16,4,2048]{2,1,0:T(4,128)(2,1)}) custom-call(s32[16]{0:T(128)} %get-tuple-element.8.pick_ref, s32[8]{0:T(128)} %compare_select_fusion.7.give_ref, bf16[16,4,6144]{2,1,0:T(4,128)(2,1)} %shard_map.204.done_ref), custom_call_target="tpu_custom_call" | custom-call | tf_op jit(solution)/shard_map/pallas_call | solution.py:326
  72.9 2.0 %copy.31 = bf16[16,4,4096]{2,1,0:T(4,128)(2,1)} copy(bf16[16,4,4096]{2,1,0:T(4,128)(2,1)} %get-tuple-element.12) | data formatting | bytes 1048576
  75.0 1.8 %copy.32 = bf16[16,4,2048]{2,1,0:T(4,128)(2,1)} copy(bf16[16,4,2048]{2,1,0:T(4,128)(2,1)} %get-tuple-element.13) | data formatting | bytes 524288
  (11 shorter events, 0.2 us)
Async XLA Ops:
  0.6 4.4 %copy-start.3 = (bf16[16,4,2,256]{3,2,1,0:T(2,128)(2,1)S(1)}, bf16[16,4,2,256]{3,2,1,0:T(2,128)(2,1)}, u32[]{:S(2)}) copy-start(bf16[16,4,2,256]{3,2,1,0:T(2,128)(2,1)} %param.30) | copy-start | bytes 196612
  0.6 4.5 %copy-start.5 = (bf16[16,4,64]{2,1,0:T(4,128)(2,1)S(1)}, bf16[16,4,64]{2,1,0:T(4,128)(2,1)}, u32[]{:S(2)}) copy-start(bf16[16,4,64]{2,1,0:T(4,128)(2,1)} %param.31) | copy-start | bytes 24580
  0.7 4.6 %copy-start.2 = (bf16[16,4,2048]{2,1,0:T(4,128)(2,1)S(1)}, bf16[16,4,2048]{2,1,0:T(4,128)(2,1)}, u32[]{:S(2)}) copy-start(bf16[16,4,2048]{2,1,0:T(4,128)(2,1)} %param.32) | copy-start | bytes 786436
  2.5 2.9 %copy-start.4 = (bf16[16,4,2,256]{3,2,1,0:T(2,128)(2,1)S(1)}, bf16[16,4,2,256]{3,2,1,0:T(2,128)(2,1)}, u32[]{:S(2)}) copy-start(bf16[16,4,2,256]{3,2,1,0:T(2,128)(2,1)} %param.33) | copy-start | bytes 196612
  2.5 3.0 %copy-start.6 = (s32[16]{0:T(128)S(1)}, s32[16]{0:T(128)}, u32[]{:S(2)}) copy-start(s32[16]{0:T(128)} %param.27) | copy-start | bytes 196
  5.1 23.4 %copy-start.7 = (s32[128]{0:T(128)S(1)}, s32[128]{0:T(128)}, u32[]{:S(2)}) copy-start(s32[128]{0:T(128)} %param.26) | copy-start | bytes 1540
  5.1 23.3 %copy-start.8 = (s32[128]{0:T(128)S(1)}, s32[128]{0:T(128)}, u32[]{:S(2)}) copy-start(s32[128]{0:T(128)} %param.25) | copy-start | bytes 1540
  5.1 24.0 %copy-start.1 = (bf16[16,3,4096]{2,0,1:T(8,128)(2,1)S(1)}, bf16[16,3,4096]{2,0,1:T(8,128)(2,1)}, u32[]{:S(2)}) copy-start(bf16[16,3,4096]{2,0,1:T(8,128)(2,1)} %param.21) | copy-start | bytes 1179652
  5.5 1.1 %copy-start = (bf16[16,4,11392]{2,1,0:T(4,128)(2,1)}, bf16[16,4,11392]{2,1,0:T(4,128)(2,1)S(1)}, u32[]{:S(2)}) copy-start(bf16[16,4,11392]{2,1,0:T(4,128)(2,1)S(1)} %constant_dynamic-update-slice_fusion.packed_ref) | copy-start | bytes 4374532
